TPU v7x, 256 devices: a whole 4x4x8 slice. The times are simulated.
256 devices in a mesh: ta: 16 (over x_lo, z), gz: 2 (over core), gy: 4 (over y), gx: 2 (over x_hi).
Axes of the slice: x: 4 (x_hi: 2, x_lo: 2; x = x_hi * 2 + x_lo), y: 4, z: 8, core: 2. Of those that a mesh axis runs over, the one named last changes fastest.
Arguments:
- source: float32 [2, 4, 3, 16, 2, 4, 8, 256], P(None, None, None, 'ta', 'gz', 'gy', 'gx'), may hold values from -6 to 6
- gauge_links: bfloat16 [4, 2, 3, 3, 16, 2, 4, 8, 256], P(None, None, None, None, 'ta', 'gz', 'gy', 'gx'), may hold values from -2.5 to 2.5
- clover_inverse: bfloat16 [2, 2, 6, 6, 16, 2, 4, 8, 256], P(None, None, None, None, 'ta', 'gz', 'gy', 'gx'), may hold values from -0.5 to 1.5, as said below
- vectors: bfloat16 [16, 2, 4, 3, 16, 2, 4, 8, 256], P(None, None, None, None, 'ta', 'gz', 'gy', 'gx'), may hold values from -0.75 to 0.75
- coarse_hops: float32 [8, 2, 16, 16, 16, 2, 4, 8], P(None, None, None, None, 'ta', 'gz', 'gy', 'gx'), may hold values from -0.25 to 0.25
Outputs:
- solution: float32 [2, 4, 3, 16, 2, 4, 8, 256], P(None, None, None, 'ta', 'gz', 'gy', 'gx')
- coarse_error: float32 [2, 16, 16, 2, 4, 8], P(None, None, 'ta', 'gz', 'gy', 'gx')
Inputs may be any that keep to these rules, and one draw needn't show every extreme that they name: `clover_inverse`: each chirality block is hermitian.
All inputs are finite; a program needn't handle non-finite values.
Results may differ from a plain program's by a relative error of at most 0.0029.
Values sent between devices are 32-bit elements; how exact they have to be, the bound alone decides.
A program may use at most 128 MiB of HBM per device.

v0:
```python
import jax
import jax.numpy as jnp
import numpy as np
from jax import lax
from jax.sharding import PartitionSpec as P

EDGE = 4


kappa_value = 0.125
fine_relax = 0.8
coarse_relax = 0.7


def extended(block, sides, width):
    for axis, dim in sides:
        count = lax.axis_size(axis)
        forward = [(i, i + 1) for i in range(count - 1)]
        forward.append((count - 1, 0))
        backward = [(target, source) for source, target in forward]
        low = lax.ppermute(
            lax.slice_in_dim(block, block.shape[dim] - width, None, axis=dim), axis, forward
        )
        high = lax.ppermute(lax.slice_in_dim(block, 0, width, axis=dim), axis, backward)
        block = jnp.concatenate([low, block, high], axis=dim)
    return block


def real_form(real_part, imag_part):
    rows, columns = real_part.shape
    result = np.zeros((2 * rows, 2 * columns), np.float32)
    result[:rows, :columns] = real_part
    result[:rows, columns:] = -imag_part
    result[rows:, :columns] = imag_part
    result[rows:, columns:] = real_part
    return result


def side_by_side(sign, coupling_real, coupling_imag):
    real_part = np.zeros((2, 4), np.float32)
    imag_part = np.zeros((2, 4), np.float32)
    real_part[:, :2] = np.eye(2, dtype=np.float32)
    real_part[:, 2:] = sign * coupling_real
    imag_part[:, 2:] = sign * coupling_imag
    return real_form(real_part, imag_part)


def one_above(sign, coupling_real, coupling_imag):
    real_part = np.zeros((4, 2), np.float32)
    imag_part = np.zeros((4, 2), np.float32)
    real_part[:2, :] = np.eye(2, dtype=np.float32)
    real_part[2:, :] = sign * coupling_real
    imag_part[2:, :] = sign * coupling_imag
    return real_form(real_part, imag_part)


def spin_tables():
    zero_block = np.zeros((2, 2), np.float32)
    couplings = [
        (np.eye(2, dtype=np.float32), zero_block),
        (zero_block, np.array([[-1.0, 0.0], [0.0, 1.0]], np.float32)),
        (np.array([[0.0, -1.0], [1.0, 0.0]], np.float32), zero_block),
        (zero_block, np.array([[0.0, -1.0], [-1.0, 0.0]], np.float32)),
    ]
    tables = []
    for coupling_real, coupling_imag in couplings:
        adjoint_real = coupling_real.T
        adjoint_imag = -coupling_imag.T
        tables.append(
            (
                side_by_side(-1.0, coupling_real, coupling_imag),
                one_above(-1.0, adjoint_real, adjoint_imag),
                side_by_side(1.0, coupling_real, coupling_imag),
                one_above(1.0, adjoint_real, adjoint_imag),
            )
        )
    return tables


def apply_spin(spin_table, spinor):
    pairs = spinor.shape[1]
    flattened = spinor.reshape((2 * pairs,) + spinor.shape[2:])
    result = jnp.tensordot(
        jnp.asarray(spin_table), flattened, axes=1, precision=lax.Precision.HIGHEST
    )
    return result.reshape((2, spin_table.shape[0] // 2) + spinor.shape[2:])


def colour(matrix, vector):
    real_part = matrix[0].astype(jnp.float32)[None]
    imag_part = matrix[1].astype(jnp.float32)[None]
    vector_real = vector[0][:, None]
    vector_imag = vector[1][:, None]
    return jnp.stack(
        [
            jnp.sum(real_part * vector_real - imag_part * vector_imag, axis=2),
            jnp.sum(real_part * vector_imag + imag_part * vector_real, axis=2),
        ]
    )


def adjoint(matrix):
    return jnp.stack([jnp.swapaxes(matrix[0], 0, 1), -jnp.swapaxes(matrix[1], 0, 1)])


def exchange_faces(payload, direction):
    if direction == 0:
        return extended(payload, (("ta", 3),), 1)
    if direction == 1:
        return extended(payload, (("gz", 4),), 1)
    if direction == 2:
        return extended(payload, (("gy", 5),), 1)
    return extended(payload, (("gx", 6),), 1)


def split_layers(values, direction):
    stride = EDGE ** (3 - direction)
    return values.reshape(values.shape[:-1] + (EDGE**direction, EDGE, stride))


def hopping(spinor, gauge_links):
    summed = jnp.zeros_like(spinor)
    tables = spin_tables()
    for direction in range(4):
        project_minus, lift_minus, project_plus, lift_plus = tables[direction]
        block_axis = 3 + direction
        link_matrix = gauge_links[direction]
        forward_half = split_layers(apply_spin(project_minus, spinor), direction)
        backward_half = split_layers(
            colour(adjoint(link_matrix), apply_spin(project_plus, spinor)), direction
        )
        layer_shape = forward_half.shape[:-3] + (EDGE**3,)
        forward_layers = forward_half[..., 0, :].reshape(layer_shape)
        backward_layers = backward_half[..., EDGE - 1, :].reshape(layer_shape)
        slab_count = forward_layers.shape[block_axis]
        payload = jnp.concatenate(
            [
                lax.slice_in_dim(forward_layers, 0, 1, axis=block_axis),
                lax.slice_in_dim(backward_layers, slab_count - 1, slab_count, axis=block_axis),
            ],
            axis=block_axis,
        )
        padded = exchange_faces(payload, direction)
        from_below = lax.slice_in_dim(padded, 0, 1, axis=block_axis)
        from_above = lax.slice_in_dim(padded, 3, 4, axis=block_axis)
        next_layers = jnp.concatenate(
            [lax.slice_in_dim(forward_layers, 1, slab_count, axis=block_axis), from_above],
            axis=block_axis,
        )
        prior_layers = jnp.concatenate(
            [from_below, lax.slice_in_dim(backward_layers, 0, slab_count - 1, axis=block_axis)],
            axis=block_axis,
        )
        single_shape = forward_half.shape[:-2] + (1, forward_half.shape[-1])
        flat_shape = forward_half.shape[:-3] + (spinor.shape[-1],)
        ahead_values = jnp.concatenate(
            [forward_half[..., 1:, :], next_layers.reshape(single_shape)], axis=-2
        )
        behind = jnp.concatenate(
            [prior_layers.reshape(single_shape), backward_half[..., : EDGE - 1, :]], axis=-2
        )
        ahead_values = ahead_values.reshape(flat_shape)
        behind = behind.reshape(flat_shape)
        summed = (
            summed
            + apply_spin(lift_minus, colour(link_matrix, ahead_values))
            + apply_spin(lift_plus, behind)
        )
    return summed


def clover_apply(clover, spinor):
    pieces = []
    for chirality in range(2):
        half_spinor = spinor[:, 2 * chirality : 2 * chirality + 2]
        flattened = half_spinor.reshape((2, 1, 6) + half_spinor.shape[3:])
        pieces.append(colour(clover[chirality], flattened).reshape(half_spinor.shape))
    return jnp.concatenate(pieces, axis=1)


def restrict(residual, vectors):
    rounded = residual.astype(jnp.bfloat16)
    stacked = jnp.stack([rounded, jnp.stack([rounded[1], -rounded[0]])])
    return jnp.einsum(
        "krsctzyxi,jrsctzyxi->jktzyx", vectors, stacked, preferred_element_type=jnp.float32
    )


def prolong(coarse_error, vectors):
    rounded = coarse_error.astype(jnp.bfloat16)
    parts = jnp.einsum(
        "krsctzyxi,jktzyx->jrsctzyxi", vectors, rounded, preferred_element_type=jnp.float32
    )
    return jnp.stack([parts[0, 0] - parts[1, 1], parts[0, 1] + parts[1, 0]])


def offset_view(padded, direction, offset):
    result = padded
    for axis_number in range(4):
        start = 1 + (offset if axis_number == direction else 0)
        result = lax.slice_in_dim(
            result, start, start + padded.shape[2 + axis_number] - 2, axis=2 + axis_number
        )
    return result


def wrap_pad(values, axis_number):
    length = values.shape[axis_number]
    return jnp.concatenate(
        [
            lax.slice_in_dim(values, length - 1, length, axis=axis_number),
            values,
            lax.slice_in_dim(values, 0, 1, axis=axis_number),
        ],
        axis=axis_number,
    )


def coarse_terms(coarse_error, coarse_hops, padded):
    summed = coarse_error
    for direction in range(4):
        ahead_values = offset_view(padded, direction, 1)
        behind = offset_view(padded, direction, -1)
        summed = summed - colour(coarse_hops[2 * direction], ahead_values[:, None])[:, 0]
        summed = summed - colour(coarse_hops[2 * direction + 1], behind[:, None])[:, 0]
    return summed


def regroup(values, time_axis, group_sizes):
    trailing = values.shape[1:]
    trailing_count = len(trailing)
    reshaped = values.reshape(group_sizes + trailing)
    permutation = [3 + index for index in range(time_axis + 1)]
    permutation = permutation + [0, 4 + time_axis, 1, 5 + time_axis, 2, 6 + time_axis]
    permutation = permutation + [3 + index for index in range(time_axis + 4, trailing_count)]
    moved = jnp.transpose(reshaped, permutation)
    merged_shape = (
        trailing[: time_axis + 1]
        + (
            group_sizes[0] * trailing[time_axis + 1],
            group_sizes[1] * trailing[time_axis + 2],
            group_sizes[2] * trailing[time_axis + 3],
        )
        + trailing[time_axis + 4 :]
    )
    return moved.reshape(merged_shape)


def local(source, gauge_links, clover_inverse, vectors, coarse_hops):

    def operator(spinor):
        return spinor - kappa_value * clover_apply(clover_inverse, hopping(spinor, gauge_links))

    iterate = fine_relax * source
    iterate = iterate + fine_relax * (source - operator(iterate))
    residual = source - operator(iterate)
    coarse_source = restrict(residual, vectors)
    grouped_source, grouped_hops = (
        lax.all_gather(coarse_source[None], ("gz", "gy", "gx"), axis=0, tiled=True),
        lax.all_gather(coarse_hops[None], ("gz", "gy", "gx"), axis=0, tiled=True),
    )
    group_sizes = (lax.axis_size("gz"), lax.axis_size("gy"), lax.axis_size("gx"))
    whole_source = regroup(grouped_source, 2, group_sizes)
    whole_hops = regroup(grouped_hops, 4, group_sizes)
    coarse_error = coarse_relax * whole_source
    padded = extended(coarse_error, (("ta", 2),), 1)
    for axis_number in (3, 4, 5):
        padded = wrap_pad(padded, axis_number)
    coarse_error = coarse_error + coarse_relax * (
        whole_source - coarse_terms(coarse_error, whole_hops, padded)
    )
    depth_blocks = coarse_source.shape[3]
    height_blocks = coarse_source.shape[4]
    width_blocks = coarse_source.shape[5]
    coarse_error = lax.dynamic_slice_in_dim(
        coarse_error, lax.axis_index("gz") * depth_blocks, depth_blocks, 3
    )
    coarse_error = lax.dynamic_slice_in_dim(
        coarse_error, lax.axis_index("gy") * height_blocks, height_blocks, 4
    )
    coarse_error = lax.dynamic_slice_in_dim(
        coarse_error, lax.axis_index("gx") * width_blocks, width_blocks, 5
    )
    iterate = iterate + prolong(coarse_error, vectors)
    for repeat in range(2):
        iterate = iterate + fine_relax * (source - operator(iterate))
    return (iterate, coarse_error)


def solution(mesh):
    return jax.shard_map(
        local,
        mesh=mesh,
        in_specs=(
            P(None, None, None, "ta", "gz", "gy", "gx", None),
            P(None, None, None, None, "ta", "gz", "gy", "gx", None),
            P(None, None, None, None, "ta", "gz", "gy", "gx", None),
            P(None, None, None, None, "ta", "gz", "gy", "gx", None),
            P(None, None, None, None, "ta", "gz", "gy", "gx"),
        ),
        out_specs=(
            P(None, None, None, "ta", "gz", "gy", "gx", None),
            P(None, None, "ta", "gz", "gy", "gx"),
        ),
        check_vma=False,
    )
```

profile of v0, /device:TPU:24, one launch (start us, length us, event | category | flops | bytes accessed | tf_op | source)
XLA Modules:
  0.0 410.2 jit_solution(18174673846398442304)
XLA Ops:
  10.4 6.8 %collective-permute-start = (f32[2,2,3,1,1,1,4,64]{7,1,0,6,2,5,4,3:T(2,128)}, f32[2,2,3,1,1,1,4,64]{7,1,0,6,2,5,4,3:T(2,128)}, u32[]{:S(2)}, u32[]{:S(2)}) collective-permute-start(f32[2,2,3,1,1,1,4,64]{7,1,0,6,2,5,4,3:T(2,128)} %bitcast.8), channel_id=1, source_target_pairs={{16,0},{32,16},{48,32},{64,48},{80,64},{96,80},{112,96},{128,112},... | collective-permute-start | bytes 36872 | tf_op jit(solution)/shard_map/ppermute | solution.py:24
  26.3 3.2 collective-permute-start.6
  29.8 3.2 reshape_reshape.66
  33.0 3.3 slice_reduce_fusion.7
  56.8 2.9 copy.1435
  71.6 2.6 collective-permute-start.5
  106.4 3.9 collective-permute-start.8
  115.0 2.0 reshape_reshape.70
  124.7 2.4 copy.1507
  131.9 2.0 copy.1526
  135.6 2.0 copy.1525
  143.2 2.9 copy.1499
  157.1 3.5 collective-permute-start.13
  176.4 2.2 copy.1786
  184.6 34.0 %all-gather = f32[32,16,1,1,1,4]{1,5,4,3,2,0:T(4,128)S(1)} all-gather(f32[2,16,1,1,1,4]{1,5,4,3,2,0:T(4,128)S(1)} %copy.1539), channel_id=2, replica_groups=mesh['ta'=16,'gz'=2,'gy'=4,'gx'=2] {'gz','gy','gx'}, dimensions={0}, use_global_device_ids=true | all-gather | bytes 8704 | tf_op jit(solution)/shard_map/all_gather | solution.py:259
  218.7 4.4 %collective-permute-start.16 = (f32[2,16,1,2,4,8]{1,5,4,3,0,2:T(8,128)S(1)}, f32[2,16,1,2,4,8]{1,5,4,3,0,2:T(8,128)S(1)}, u32[]{:S(2)}, u32[]{:S(2)}) collective-permute-start(f32[2,16,1,2,4,8]{1,5,4,3,0,2:T(8,128)S(1)} %broadcast_multiply_fusion), channel_id=1, source_target_pairs={{16,0},{32,16},{48,32},{64,48},{80,64},{96,80},{112,96},{128,112},... | collective-permute-start | bytes 24584 | tf_op jit(solution)/shard_map/ppermute | solution.py:24
  225.0 4.7 %collective-permute-done.17 = f32[2,16,1,2,4,8]{1,5,4,3,0,2:T(8,128)S(1)} collective-permute-done((f32[2,16,1,2,4,8]{1,5,4,3,0,2:T(8,128)S(1)}, f32[2,16,1,2,4,8]{1,5,4,3,0,2:T(8,128)S(1)}, u32[]{:S(2)}, u32[]{:S(2)}) %collective-permute-start.17) | collective-permute-done | bytes 8224 | tf_op jit(solution)/shard_map/ppermute | solution.py:21
  232.0 10.8 %copy.2038 = f32[2,4,2,8,2,16,16,1,1,1,4]{6,10,5,4,3,2,1,0,9,8,7:T(4,128)} copy(f32[2,4,2,8,2,16,16,1,1,1,4]{6,5,10,4,3,2,1,0,9,8,7:T(8,128)} %bitcast.860) | data formatting | bytes 2097152 | tf_op jit(solution)/shard_map/reshape | solution.py:232
  242.9 3.6 subtract_reduce_fusion.3
  247.2 3.6 subtract_reduce_fusion.4
  251.1 2.7 subtract_reduce_fusion.6
  292.4 2.9 copy.1599
  297.8 3.1 collective-permute-start.25
  306.8 3.5 collective-permute-start.23
  337.5 3.2 reshape_reshape.78
  340.7 3.3 slice.1406
  344.0 3.3 slice_reduce_fusion.4
  348.6 2.1 collective-permute-start.26
  359.8 3.4 collective-permute-start.33
  364.8 2.1 copy.1675
  371.1 4.2 %collective-permute-done.32 = f32[2,2,3,1,1,1,1,64]{7,6,2,1,0,5,4,3:T(1,128)S(1)} collective-permute-done((f32[2,2,3,1,1,1,1,64]{7,6,2,1,0,5,4,3:T(1,128)S(1)}, f32[2,2,3,1,1,1,1,64]{7,6,2,1,0,5,4,3:T(1,128)S(1)}, u32[]{:S(2)}, u32[]{:S(2)}) %collective-permute-start.32) | collective-permute-done | bytes 3104 | tf_op jit(solution)/shard_map/ppermute | solution.py:24
  381.3 3.4 collective-permute-start.31
  (1092 shorter events, 249.0 us)
Async XLA Ops:
  7.2 224.7 %all-gather.4.cloned.1.call-start = ((), (), s32[]{:S(2)}) async-start(), calls=%async_computation | async-start | bytes 8912896 | tf_op jit(solution)/shard_map/all_gather | solution.py:260
  10.4 69.7 %collective-permute-start = (f32[2,2,3,1,1,1,4,64]{7,1,0,6,2,5,4,3:T(2,128)}, f32[2,2,3,1,1,1,4,64]{7,1,0,6,2,5,4,3:T(2,128)}, u32[]{:S(2)}, u32[]{:S(2)}) collective-permute-start(f32[2,2,3,1,1,1,4,64]{7,1,0,6,2,5,4,3:T(2,128)} %bitcast.8), channel_id=1, source_target_pairs={{16,0},{32,16},{48,32},{64,48},{80,64},{96,80},{112,96},{128,112},... | collective-permute-start | bytes 36872 | tf_op jit(solution)/shard_map/ppermute | solution.py:24
  19.3 57.3 %collective-permute-start.1 = (f32[2,2,3,1,1,1,4,64]{7,1,0,6,2,5,4,3:T(2,128)}, f32[2,2,3,1,1,1,4,64]{7,1,0,6,2,5,4,3:T(2,128)}, u32[]{:S(2)}, u32[]{:S(2)}) collective-permute-start(f32[2,2,3,1,1,1,4,64]{7,1,0,6,2,5,4,3:T(2,128)} %bitcast.26), channel_id=1, source_target_pairs={{0,16},{16,32},{32,48},{48,64},{64,80},{80,96},{96,112},{112,128},... | collective-permute-start | bytes 36872 | tf_op jit(solution)/shard_map/ppermute | solution.py:21
  20.9 57.8 %collective-permute-start.2 = (f32[2,2,3,1,1,1,4,64]{7,1,0,6,2,5,4,3:T(2,128)}, f32[2,2,3,1,1,1,4,64]{7,1,0,6,2,5,4,3:T(2,128)}, u32[]{:S(2)}, u32[]{:S(2)}) collective-permute-start(f32[2,2,3,1,1,1,4,64]{7,1,0,6,2,5,4,3:T(2,128)} %reshape_squeeze.98), channel_id=1, source_target_pairs={{8,0},{0,8},{9,1},{1,9},{10,2},{2,10},{11,3},{3,11},{12,4},{4,12},... | collective-permute-start | bytes 36872 | tf_op jit(solution)/shard_map/ppermute | solution.py:24
  22.8 48.9 %collective-permute-start.3 = (f32[2,2,3,1,1,1,4,64]{7,1,0,6,2,5,4,3:T(2,128)}, f32[2,2,3,1,1,1,4,64]{7,1,0,6,2,5,4,3:T(2,128)}, u32[]{:S(2)}, u32[]{:S(2)}) collective-permute-start(f32[2,2,3,1,1,1,4,64]{7,1,0,6,2,5,4,3:T(2,128)} %copy.1849), channel_id=1, source_target_pairs={{0,8},{8,0},{1,9},{9,1},{2,10},{10,2},{3,11},{11,3},{4,12},{12,4},... | collective-permute-start | bytes 36872 | tf_op jit(solution)/shard_map/ppermute | solution.py:21
  26.3 36.1 %collective-permute-start.6 = (f32[2,2,3,1,1,1,1,64]{7,6,2,1,0,5,4,3:T(1,128)}, f32[2,2,3,1,1,1,1,64]{7,6,2,1,0,5,4,3:T(1,128)}, u32[]{:S(2)}, u32[]{:S(2)}) collective-permute-start(f32[2,2,3,1,1,1,1,64]{7,6,2,1,0,5,4,3:T(1,128)} %slice.1274), channel_id=1, source_target_pairs={{1,0},{0,1},{3,2},{2,3},{5,4},{4,5},{7,6},{6,7},{9,8},{8,9},{11,10... | collective-permute-start | bytes 9224 | tf_op jit(solution)/shard_map/ppermute | solution.py:24
  67.8 9.6 %collective-permute-start.4 = (f32[2,2,3,1,1,1,4,64]{7,6,2,1,0,5,4,3:T(4,128)}, f32[2,2,3,1,1,1,4,64]{7,6,2,1,0,5,4,3:T(4,128)}, u32[]{:S(2)}, u32[]{:S(2)}) collective-permute-start(f32[2,2,3,1,1,1,4,64]{7,6,2,1,0,5,4,3:T(4,128)} %reshape_squeeze.100), channel_id=1, source_target_pairs={{2,0},{4,2},{6,4},{0,6},{3,1},{5,3},{7,5},{1,7},{10,8},{12,10},{14... | collective-permute-start | bytes 36872 | tf_op jit(solution)/shard_map/ppermute | solution.py:24
  71.6 16.6 %collective-permute-start.5 = (f32[2,2,3,1,1,1,4,64]{7,6,2,1,0,5,4,3:T(4,128)}, f32[2,2,3,1,1,1,4,64]{7,6,2,1,0,5,4,3:T(4,128)S(1)}, u32[]{:S(2)}, u32[]{:S(2)}) collective-permute-start(f32[2,2,3,1,1,1,4,64]{7,6,2,1,0,5,4,3:T(4,128)} %reshape_squeeze.101), channel_id=1, source_target_pairs={{0,2},{2,4},{4,6},{6,0},{1,3},{3,5},{5,7},{7,1},{8,10},{10,12},{12... | collective-permute-start | bytes 36872 | tf_op jit(solution)/shard_map/ppermute | solution.py:21
  106.4 54.9 %collective-permute-start.8 = (f32[2,2,3,1,1,1,4,64]{7,1,0,6,2,5,4,3:T(2,128)}, f32[2,2,3,1,1,1,4,64]{7,1,0,6,2,5,4,3:T(2,128)}, u32[]{:S(2)}, u32[]{:S(2)}) collective-permute-start(f32[2,2,3,1,1,1,4,64]{7,1,0,6,2,5,4,3:T(2,128)} %bitcast.121), channel_id=1, source_target_pairs={{16,0},{32,16},{48,32},{64,48},{80,64},{96,80},{112,96},{128,112},... | collective-permute-start | bytes 36872 | tf_op jit(solution)/shard_map/ppermute | solution.py:24
  111.4 45.7 %collective-permute-start.9 = (f32[2,2,3,1,1,1,4,64]{7,1,0,6,2,5,4,3:T(2,128)}, f32[2,2,3,1,1,1,4,64]{7,1,0,6,2,5,4,3:T(2,128)}, u32[]{:S(2)}, u32[]{:S(2)}) collective-permute-start(f32[2,2,3,1,1,1,4,64]{7,1,0,6,2,5,4,3:T(2,128)} %bitcast.130), channel_id=1, source_target_pairs={{0,16},{16,32},{32,48},{48,64},{64,80},{80,96},{96,112},{112,128},... | collective-permute-start | bytes 36872 | tf_op jit(solution)/shard_map/ppermute | solution.py:21
  112.8 54.2 %collective-permute-start.10 = (f32[2,2,3,1,1,1,4,64]{7,1,0,6,2,5,4,3:T(2,128)}, f32[2,2,3,1,1,1,4,64]{7,1,0,6,2,5,4,3:T(2,128)}, u32[]{:S(2)}, u32[]{:S(2)}) collective-permute-start(f32[2,2,3,1,1,1,4,64]{7,1,0,6,2,5,4,3:T(2,128)} %reshape_squeeze.106), channel_id=1, source_target_pairs={{8,0},{0,8},{9,1},{1,9},{10,2},{2,10},{11,3},{3,11},{12,4},{4,12},... | collective-permute-start | bytes 36872 | tf_op jit(solution)/shard_map/ppermute | solution.py:24
  114.4 48.0 %collective-permute-start.11 = (f32[2,2,3,1,1,1,4,64]{7,1,0,6,2,5,4,3:T(2,128)}, f32[2,2,3,1,1,1,4,64]{7,1,0,6,2,5,4,3:T(2,128)}, u32[]{:S(2)}, u32[]{:S(2)}) collective-permute-start(f32[2,2,3,1,1,1,4,64]{7,1,0,6,2,5,4,3:T(2,128)} %copy.1850), channel_id=1, source_target_pairs={{0,8},{8,0},{1,9},{9,1},{2,10},{10,2},{3,11},{11,3},{4,12},{12,4},... | collective-permute-start | bytes 36872 | tf_op jit(solution)/shard_map/ppermute | solution.py:21
  127.1 21.6 %collective-permute-start.14 = (f32[2,2,3,1,1,1,1,64]{7,6,2,1,0,5,4,3:T(1,128)}, f32[2,2,3,1,1,1,1,64]{7,6,2,1,0,5,4,3:T(1,128)S(1)}, u32[]{:S(2)}, u32[]{:S(2)}) collective-permute-start(f32[2,2,3,1,1,1,1,64]{7,6,2,1,0,5,4,3:T(1,128)} %slice.1311), channel_id=1, source_target_pairs={{1,0},{0,1},{3,2},{2,3},{5,4},{4,5},{7,6},{6,7},{9,8},{8,9},{11,10... | collective-permute-start | bytes 9224 | tf_op jit(solution)/shard_map/ppermute | solution.py:24
  153.9 11.8 %collective-permute-start.12 = (f32[2,2,3,1,1,1,4,64]{7,6,2,1,0,5,4,3:T(4,128)}, f32[2,2,3,1,1,1,4,64]{7,6,2,1,0,5,4,3:T(4,128)}, u32[]{:S(2)}, u32[]{:S(2)}) collective-permute-start(f32[2,2,3,1,1,1,4,64]{7,6,2,1,0,5,4,3:T(4,128)} %reshape_squeeze.108), channel_id=1, source_target_pairs={{2,0},{4,2},{6,4},{0,6},{3,1},{5,3},{7,5},{1,7},{10,8},{12,10},{14... | collective-permute-start | bytes 36872 | tf_op jit(solution)/shard_map/ppermute | solution.py:24
  157.1 17.9 %collective-permute-start.13 = (f32[2,2,3,1,1,1,4,64]{7,6,2,1,0,5,4,3:T(4,128)}, f32[2,2,3,1,1,1,4,64]{7,6,2,1,0,5,4,3:T(4,128)S(1)}, u32[]{:S(2)}, u32[]{:S(2)}) collective-permute-start(f32[2,2,3,1,1,1,4,64]{7,6,2,1,0,5,4,3:T(4,128)} %reshape_squeeze.109), channel_id=1, source_target_pairs={{0,2},{2,4},{4,6},{6,0},{1,3},{3,5},{5,7},{7,1},{8,10},{10,12},{12... | collective-permute-start | bytes 36872 | tf_op jit(solution)/shard_map/ppermute | solution.py:21
  218.7 6.3 %collective-permute-start.16 = (f32[2,16,1,2,4,8]{1,5,4,3,0,2:T(8,128)S(1)}, f32[2,16,1,2,4,8]{1,5,4,3,0,2:T(8,128)S(1)}, u32[]{:S(2)}, u32[]{:S(2)}) collective-permute-start(f32[2,16,1,2,4,8]{1,5,4,3,0,2:T(8,128)S(1)} %broadcast_multiply_fusion), channel_id=1, source_target_pairs={{16,0},{32,16},{48,32},{64,48},{80,64},{96,80},{112,96},{128,112},... | collective-permute-start | bytes 24584 | tf_op jit(solution)/shard_map/ppermute | solution.py:24
  223.1 6.6 %collective-permute-start.17 = (f32[2,16,1,2,4,8]{1,5,4,3,0,2:T(8,128)S(1)}, f32[2,16,1,2,4,8]{1,5,4,3,0,2:T(8,128)S(1)}, u32[]{:S(2)}, u32[]{:S(2)}) collective-permute-start(f32[2,16,1,2,4,8]{1,5,4,3,0,2:T(8,128)S(1)} %broadcast_multiply_fusion), channel_id=1, source_target_pairs={{0,16},{16,32},{32,48},{48,64},{64,80},{80,96},{96,112},{112,128},... | collective-permute-start | bytes 24584 | tf_op jit(solution)/shard_map/ppermute | solution.py:21
  266.3 44.7 %collective-permute-start.18 = (f32[2,2,3,1,1,1,4,64]{7,1,0,6,2,5,4,3:T(2,128)}, f32[2,2,3,1,1,1,4,64]{7,1,0,6,2,5,4,3:T(2,128)}, u32[]{:S(2)}, u32[]{:S(2)}) collective-permute-start(f32[2,2,3,1,1,1,4,64]{7,1,0,6,2,5,4,3:T(2,128)} %bitcast.254), channel_id=1, source_target_pairs={{16,0},{32,16},{48,32},{64,48},{80,64},{96,80},{112,96},{128,112},... | collective-permute-start | bytes 36872 | tf_op jit(solution)/shard_map/ppermute | solution.py:24
  267.4 39.4 %collective-permute-start.19 = (f32[2,2,3,1,1,1,4,64]{7,1,0,6,2,5,4,3:T(2,128)}, f32[2,2,3,1,1,1,4,64]{7,1,0,6,2,5,4,3:T(2,128)}, u32[]{:S(2)}, u32[]{:S(2)}) collective-permute-start(f32[2,2,3,1,1,1,4,64]{7,1,0,6,2,5,4,3:T(2,128)} %bitcast.261), channel_id=1, source_target_pairs={{0,16},{16,32},{32,48},{48,64},{64,80},{80,96},{96,112},{112,128},... | collective-permute-start | bytes 36872 | tf_op jit(solution)/shard_map/ppermute | solution.py:21
  270.7 44.9 %collective-permute-start.20 = (f32[2,2,3,1,1,1,4,64]{7,1,0,6,2,5,4,3:T(2,128)}, f32[2,2,3,1,1,1,4,64]{7,1,0,6,2,5,4,3:T(2,128)}, u32[]{:S(2)}, u32[]{:S(2)}) collective-permute-start(f32[2,2,3,1,1,1,4,64]{7,1,0,6,2,5,4,3:T(2,128)} %reshape_squeeze.114), channel_id=1, source_target_pairs={{8,0},{0,8},{9,1},{1,9},{10,2},{2,10},{11,3},{3,11},{12,4},{4,12},... | collective-permute-start | bytes 36872 | tf_op jit(solution)/shard_map/ppermute | solution.py:24
  272.4 39.7 %collective-permute-start.21 = (f32[2,2,3,1,1,1,4,64]{7,1,0,6,2,5,4,3:T(2,128)}, f32[2,2,3,1,1,1,4,64]{7,1,0,6,2,5,4,3:T(2,128)}, u32[]{:S(2)}, u32[]{:S(2)}) collective-permute-start(f32[2,2,3,1,1,1,4,64]{7,1,0,6,2,5,4,3:T(2,128)} %copy.1851), channel_id=1, source_target_pairs={{0,8},{8,0},{1,9},{9,1},{2,10},{10,2},{3,11},{11,3},{4,12},{12,4},... | collective-permute-start | bytes 36872 | tf_op jit(solution)/shard_map/ppermute | solution.py:21
  281.0 16.8 %collective-permute-start.24 = (f32[2,2,3,1,1,1,1,64]{7,6,2,1,0,5,4,3:T(1,128)}, f32[2,2,3,1,1,1,1,64]{7,6,2,1,0,5,4,3:T(1,128)}, u32[]{:S(2)}, u32[]{:S(2)}) collective-permute-start(f32[2,2,3,1,1,1,1,64]{7,6,2,1,0,5,4,3:T(1,128)} %slice.1379), channel_id=1, source_target_pairs={{1,0},{0,1},{3,2},{2,3},{5,4},{4,5},{7,6},{6,7},{9,8},{8,9},{11,10... | collective-permute-start | bytes 9224 | tf_op jit(solution)/shard_map/ppermute | solution.py:24
  297.8 5.4 %collective-permute-start.25 = (f32[2,2,3,1,1,1,1,64]{7,6,2,1,0,5,4,3:T(1,128)S(1)}, f32[2,2,3,1,1,1,1,64]{7,6,2,1,0,5,4,3:T(1,128)S(1)}, u32[]{:S(2)}, u32[]{:S(2)}) collective-permute-start(f32[2,2,3,1,1,1,1,64]{7,6,2,1,0,5,4,3:T(1,128)S(1)} %slice.1384), channel_id=1, source_target_pairs={{0,1},{1,0},{2,3},{3,2},{4,5},{5,4},{6,7},{7,6},{8,9},{9,8},{10,11... | collective-permute-start | bytes 9224 | tf_op jit(solution)/shard_map/ppermute | solution.py:21
  303.3 11.0 %collective-permute-start.22 = (f32[2,2,3,1,1,1,4,64]{7,6,2,1,0,5,4,3:T(4,128)}, f32[2,2,3,1,1,1,4,64]{7,6,2,1,0,5,4,3:T(4,128)}, u32[]{:S(2)}, u32[]{:S(2)}) collective-permute-start(f32[2,2,3,1,1,1,4,64]{7,6,2,1,0,5,4,3:T(4,128)} %reshape_squeeze.116), channel_id=1, source_target_pairs={{2,0},{4,2},{6,4},{0,6},{3,1},{5,3},{7,5},{1,7},{10,8},{12,10},{14... | collective-permute-start | bytes 36872 | tf_op jit(solution)/shard_map/ppermute | solution.py:24
  306.8 16.2 %collective-permute-start.23 = (f32[2,2,3,1,1,1,4,64]{7,6,2,1,0,5,4,3:T(4,128)}, f32[2,2,3,1,1,1,4,64]{7,6,2,1,0,5,4,3:T(4,128)S(1)}, u32[]{:S(2)}, u32[]{:S(2)}) collective-permute-start(f32[2,2,3,1,1,1,4,64]{7,6,2,1,0,5,4,3:T(4,128)} %reshape_squeeze.117), channel_id=1, source_target_pairs={{0,2},{2,4},{4,6},{6,0},{1,3},{3,5},{5,7},{7,1},{8,10},{10,12},{12... | collective-permute-start | bytes 36872 | tf_op jit(solution)/shard_map/ppermute | solution.py:21
  348.6 37.2 %collective-permute-start.28 = (f32[2,2,3,1,1,1,4,64]{7,1,0,6,2,5,4,3:T(2,128)}, f32[2,2,3,1,1,1,4,64]{7,1,0,6,2,5,4,3:T(2,128)}, u32[]{:S(2)}, u32[]{:S(2)}) collective-permute-start(f32[2,2,3,1,1,1,4,64]{7,1,0,6,2,5,4,3:T(2,128)} %reshape_squeeze.122), channel_id=1, source_target_pairs={{8,0},{0,8},{9,1},{1,9},{10,2},{2,10},{11,3},{3,11},{12,4},{4,12},... | collective-permute-start | bytes 36872 | tf_op jit(solution)/shard_map/ppermute | solution.py:24
  348.6 38.4 %collective-permute-start.26 = (f32[2,2,3,1,1,1,4,64]{7,1,0,6,2,5,4,3:T(2,128)}, f32[2,2,3,1,1,1,4,64]{7,1,0,6,2,5,4,3:T(2,128)}, u32[]{:S(2)}, u32[]{:S(2)}) collective-permute-start(f32[2,2,3,1,1,1,4,64]{7,1,0,6,2,5,4,3:T(2,128)} %bitcast.297), channel_id=1, source_target_pairs={{16,0},{32,16},{48,32},{64,48},{80,64},{96,80},{112,96},{128,112},... | collective-permute-start | bytes 36872 | tf_op jit(solution)/shard_map/ppermute | solution.py:24
  351.7 29.6 %collective-permute-start.27 = (f32[2,2,3,1,1,1,4,64]{7,1,0,6,2,5,4,3:T(2,128)}, f32[2,2,3,1,1,1,4,64]{7,1,0,6,2,5,4,3:T(2,128)}, u32[]{:S(2)}, u32[]{:S(2)}) collective-permute-start(f32[2,2,3,1,1,1,4,64]{7,1,0,6,2,5,4,3:T(2,128)} %bitcast.304), channel_id=1, source_target_pairs={{0,16},{16,32},{32,48},{48,64},{64,80},{80,96},{96,112},{112,128},... | collective-permute-start | bytes 36872 | tf_op jit(solution)/shard_map/ppermute | solution.py:21
  353.5 34.8 %collective-permute-start.29 = (f32[2,2,3,1,1,1,4,64]{7,1,0,6,2,5,4,3:T(2,128)}, f32[2,2,3,1,1,1,4,64]{7,1,0,6,2,5,4,3:T(2,128)}, u32[]{:S(2)}, u32[]{:S(2)}) collective-permute-start(f32[2,2,3,1,1,1,4,64]{7,1,0,6,2,5,4,3:T(2,128)} %copy.1852), channel_id=1, source_target_pairs={{0,8},{8,0},{1,9},{9,1},{2,10},{10,2},{3,11},{11,3},{4,12},{12,4},... | collective-permute-start | bytes 36872 | tf_op jit(solution)/shard_map/ppermute | solution.py:21
  359.8 10.3 %collective-permute-start.33 = (f32[2,2,3,1,1,1,1,64]{7,6,2,1,0,5,4,3:T(1,128)S(1)}, f32[2,2,3,1,1,1,1,64]{7,6,2,1,0,5,4,3:T(1,128)S(1)}, u32[]{:S(2)}, u32[]{:S(2)}) collective-permute-start(f32[2,2,3,1,1,1,1,64]{7,6,2,1,0,5,4,3:T(1,128)S(1)} %slice.1420), channel_id=1, source_target_pairs={{0,1},{1,0},{2,3},{3,2},{4,5},{5,4},{6,7},{7,6},{8,9},{9,8},{10,11... | collective-permute-start | bytes 9224 | tf_op jit(solution)/shard_map/ppermute | solution.py:21
  375.2 16.1 %collective-permute-start.30 = (f32[2,2,3,1,1,1,4,64]{7,6,2,1,0,5,4,3:T(4,128)}, f32[2,2,3,1,1,1,4,64]{7,6,2,1,0,5,4,3:T(4,128)}, u32[]{:S(2)}, u32[]{:S(2)}) collective-permute-start(f32[2,2,3,1,1,1,4,64]{7,6,2,1,0,5,4,3:T(4,128)} %reshape_squeeze.124), channel_id=1, source_target_pairs={{2,0},{4,2},{6,4},{0,6},{3,1},{5,3},{7,5},{1,7},{10,8},{12,10},{14... | collective-permute-start | bytes 36872 | tf_op jit(solution)/shard_map/ppermute | solution.py:24
  381.3 14.7 %collective-permute-start.31 = (f32[2,2,3,1,1,1,4,64]{7,6,2,1,0,5,4,3:T(4,128)}, f32[2,2,3,1,1,1,4,64]{7,6,2,1,0,5,4,3:T(4,128)S(1)}, u32[]{:S(2)}, u32[]{:S(2)}) collective-permute-start(f32[2,2,3,1,1,1,4,64]{7,6,2,1,0,5,4,3:T(4,128)} %reshape_squeeze.125), channel_id=1, source_target_pairs={{0,2},{2,4},{4,6},{6,0},{1,3},{3,5},{5,7},{7,1},{8,10},{10,12},{12... | collective-permute-start | bytes 36872 | tf_op jit(solution)/shard_map/ppermute | solution.py:21
  (242 other events, 1116.6 us)
Sparse Core Ops, SparseCore 0:
  10.8 78.9 all-gather.3
where the time goes:
time: 418 us; the launch traced here: 410 us
  local copies, waits for them, and re-layouts  223 us (53%)
  starting transfers between devices  50.7 us (12%)
  other arithmetic  44.4 us (11%)
  blocking collectives  34 us (8%)
  matrix products  23.5 us (6%)
  between operations  19.9 us (5%)
  waiting for transfers between devices  14.5 us (3%)
    another operation x56, local copies, waits for them, and re-layouts, colour(): jnp.stack([jnp.sum(real_part * vector_real - imag_part * vector_imag, axi...  40.7 us
    slice x24, local copies, waits for them, and re-layouts, hopping(): forward_half[..., 1:, :]  34.5 us
    all_gather x1, blocking collectives, local(): lax.all_gather(coarse_source[None], ('gz', 'gy', 'gx'), axis=0, tiled=True)  34 us
    another operation x24, local copies, waits for them, and re-layouts  28.3 us
    ppermute x17, starting transfers between devices, extended(): lax.ppermute(lax.slice_in_dim(block, block.shape[dim] - width, None, axis...  26.2 us
    ppermute x17, starting transfers between devices, extended(): lax.ppermute(lax.slice_in_dim(block, 0, width, axis=dim), axis, backward)  24.5 us
    dot_general x64, matrix products, apply_spin(): jnp.tensordot(jnp.asarray(spin_table), flattened, axes=1, precision=lax.P...  21.7 us
    another operation x16, local copies, waits for them, and re-layouts, split_layers(): return values.reshape(values.shape[:-1] + (EDGE ** direction, EDGE, stride))  18.7 us
  transfers between devices with their start and end apart: 35, of which 5 were waited for; matrix products, arithmetic and copies ran while one was open for 54% of the time, Pallas kernels for 0%

commit v1 on v0

v1 whole, which is shorter than its diff:
```python
import jax
import jax.numpy as jnp
from jax import lax
from jax.experimental import pallas as pl
from jax.experimental.pallas import tpu as pltpu
from jax.sharding import PartitionSpec as P


kappa_value = 0.125
fine_relax = 0.8
coarse_relax = 0.7

F32 = jnp.float32
BF16 = jnp.bfloat16

B_ROWS = (((0, 0), (1, 0)), ((0, 3), (1, 1)), ((1, 2), (0, 0)), ((1, 3), (0, 3)))
B_ADJOINT_ROWS = (((0, 0), (1, 0)), ((0, 1), (1, 3)), ((1, 0), (0, 2)), ((1, 1), (0, 1)))

T_AHEAD, T_BEHIND, Y_AHEAD, Y_BEHIND, Z_BOTH, X_BOTH = 0, 3, 6, 9, 12, 18
TILES = 21


def plus_unit(target, unit, value):
    if unit == 0:
        return target[0] + value[0], target[1] + value[1]
    if unit == 1:
        return target[0] - value[1], target[1] + value[0]
    if unit == 2:
        return target[0] - value[0], target[1] - value[1]
    return target[0] + value[1], target[1] - value[0]


def project(spins, direction, sign):
    halves = []
    for row in range(2):
        column, unit = B_ROWS[direction][row]
        unit = unit if sign > 0 else (unit + 2) % 4
        halves.append(plus_unit(spins[row], unit, spins[2 + column]))
    return jnp.concatenate([halves[0][0], halves[1][0], halves[0][1], halves[1][1]], axis=0)


def lift(summed, half, direction, sign):
    pair = [(half[0:3], half[6:9]), (half[3:6], half[9:12])]
    result = []
    for row in range(2):
        result.append(plus_unit(summed[row], 0, pair[row]))
    for row in range(2):
        column, unit = B_ADJOINT_ROWS[direction][row]
        unit = unit if sign > 0 else (unit + 2) % 4
        result.append(plus_unit(summed[2 + row], unit, pair[column]))
    return result


def link_times(links, direction, half, dagger):
    real_part = half[:6].reshape(2, 3, 8, 128)
    imag_part = half[6:].reshape(2, 3, 8, 128)
    out_real = out_imag = None
    for b in range(3):
        if dagger:
            u_real, u_imag = links[direction, 0, b], links[direction, 1, b]
        else:
            u_real, u_imag = links[direction, 0, :, b], links[direction, 1, :, b]
        u_real, u_imag = u_real[None], u_imag[None]
        v_real, v_imag = real_part[:, b][:, None], imag_part[:, b][:, None]
        if dagger:
            term_real = u_real * v_real + u_imag * v_imag
            term_imag = u_real * v_imag - u_imag * v_real
        else:
            term_real = u_real * v_real - u_imag * v_imag
            term_imag = u_real * v_imag + u_imag * v_real
        out_real = term_real if out_real is None else out_real + term_real
        out_imag = term_imag if out_imag is None else out_imag + term_imag
    return jnp.concatenate([out_real.reshape(6, 8, 128), out_imag.reshape(6, 8, 128)], axis=0)


def lane_roll(values, shift):
    shift = shift % 128
    return values if shift == 0 else pltpu.roll(values, shift, values.ndim - 1)


def row_roll(values, shift):
    shift = shift % 8
    return values if shift == 0 else pltpu.roll(values, shift, values.ndim - 2)


class Places:
    def __init__(self):
        row = lax.broadcasted_iota(jnp.int32, (8, 128), 0)
        lane = lax.broadcasted_iota(jnp.int32, (8, 128), 1)
        self.row, self.lane = row, lane
        self.block = row % 4
        self.half = row // 4
        self.parity = lane // 64
        self.slot = {1: (lane // 16) % 4, 2: (lane // 4) % 4, 3: lane % 4}


STRIDE = {1: 16, 2: 4, 3: 1}


def choose(mask, first, second):
    return jnp.where(jnp.broadcast_to(mask[None], first.shape), first, second)


def pack_slots(half, direction, ahead, places):
    stride, slot = STRIDE[direction], places.slot[direction]
    fours = half.reshape(3, 4, 8, 128)
    packed = fours[:, 0]
    for k in range(1, 4):
        if ahead:
            packed = choose(slot == k, lane_roll(fours[:, k], stride * k), packed)
        else:
            packed = choose(slot == 3 - k, lane_roll(fours[:, k], -stride * k), packed)
    return packed


def merge_slots(rolled, packed, direction, ahead, places):
    stride, slot = STRIDE[direction], places.slot[direction]
    fours = rolled.reshape(3, 4, 8, 128)
    merged = []
    for k in range(4):
        if ahead:
            merged.append(choose(slot == 3, lane_roll(packed, stride * (3 - k)), fours[:, k]))
        else:
            merged.append(choose(slot == 0, lane_roll(packed, -stride * (3 - k)), fours[:, k]))
    return jnp.stack(merged, axis=1).reshape(12, 8, 128)


def pack_time(half, ahead, places):
    edge = places.parity == (0 if ahead else 1)
    edge_rows = places.half == (0 if ahead else 1)
    pairs = half.reshape(6, 2, 8, 128)
    first, second = pairs[:, 0], lane_roll(pairs[:, 1], 64)
    paired = choose(edge, first, second).reshape(3, 2, 8, 128)
    paired_first, paired_second = paired[:, 0], row_roll(paired[:, 1], 4)
    packed = choose(edge_rows, paired_first, paired_second)
    return packed, (first, second, paired_first, paired_second)


def merge_time(state, packed, ahead, places):
    edge = places.parity == (0 if ahead else 1)
    edge_rows = places.half == (0 if ahead else 1)
    first, second, paired_first, paired_second = state
    next_first = row_roll(choose(edge_rows, packed, paired_first), 4)
    next_second = choose(edge_rows, paired_second, packed)
    moved = jnp.stack([next_first, next_second], axis=1).reshape(6, 8, 128)
    out_first = lane_roll(choose(edge, moved, first), 64)
    out_second = choose(edge, second, moved)
    return jnp.stack([out_first, out_second], axis=1).reshape(12, 8, 128)


def spins_of(values):
    return [(values[3 * s : 3 * s + 3], values[12 + 3 * s : 15 + 3 * s]) for s in range(4)]


def tiles_of(spins):
    return jnp.concatenate([spin[0] for spin in spins] + [spin[1] for spin in spins], axis=0)


def kernel(
    source_hbm,
    links_hbm,
    clover_hbm,
    vectors_hbm,
    hops_hbm,
    out_ref,
    coarse_ref,
    source_ref,
    links_raw,
    clover_raw,
    vectors_raw,
    hops_ref,
    links,
    clover,
    matrix,
    scaled,
    send_buffer,
    recv_buffer,
    coarse_send,
    coarse_recv,
    load_sem,
    send_sem,
    recv_sem,
    coarse_send_sem,
    coarse_recv_sem,
):
    loads = []
    for index, (origin, target) in enumerate(
        (
            (source_hbm, source_ref),
            (links_hbm, links_raw),
            (clover_hbm, clover_raw),
            (vectors_hbm, vectors_raw),
            (hops_hbm, hops_ref),
        )
    ):
        loads.append(pltpu.make_async_copy(origin, target, load_sem.at[index]))
        loads[-1].start()

    def around(axis, step):
        count = lax.axis_size(axis)
        return {axis: lax.rem(lax.axis_index(axis) + (step + count), count)}

    t_next, t_prior = around("ta", 1), around("ta", -1)
    y_next, y_prior = around("gy", 1), around("gy", -1)
    z_other, x_other = around("gz", 1), around("gx", 1)

    barrier = pltpu.get_barrier_semaphore()
    for neighbour in (t_next, t_prior, y_next, y_prior, z_other, x_other):
        pl.semaphore_signal(
            barrier, inc=1, device_id=neighbour, device_id_type=pl.DeviceIdType.MESH
        )

    places = Places()

    def message(sweep, number, start, count, target):
        window = pl.ds(start, count)
        return pltpu.make_async_remote_copy(
            src_ref=send_buffer.at[sweep, window],
            dst_ref=recv_buffer.at[sweep, window],
            send_sem=send_sem.at[sweep, number],
            recv_sem=recv_sem.at[sweep, number],
            device_id=target,
            device_id_type=pl.DeviceIdType.MESH,
        )

    started = []

    def clover_hopping(sweep, psi, before_send=None, while_waiting=None):
        spins = spins_of(psi)
        send = send_buffer.at[sweep]
        recv = recv_buffer.at[sweep]
        ahead = [project(spins, mu, -1) for mu in range(4)]
        behind = [link_times(links, mu, project(spins, mu, 1), True) for mu in range(4)]

        x_ahead = pack_slots(ahead[3], 3, True, places)
        x_behind = pack_slots(behind[3], 3, False, places)
        send[X_BOTH : X_BOTH + 3] = choose(places.block == 0, x_ahead, x_behind)
        t_ahead, t_ahead_state = pack_time(ahead[0], True, places)
        send[T_AHEAD : T_AHEAD + 3] = t_ahead
        t_behind, t_behind_state = pack_time(behind[0], False, places)
        send[T_BEHIND : T_BEHIND + 3] = t_behind
        send[Y_AHEAD : Y_AHEAD + 3] = pack_slots(ahead[2], 2, True, places)
        send[Y_BEHIND : Y_BEHIND + 3] = pack_slots(behind[2], 2, False, places)
        send[Z_BOTH : Z_BOTH + 3] = pack_slots(ahead[1], 1, True, places)
        send[Z_BOTH + 3 : Z_BOTH + 6] = pack_slots(behind[1], 1, False, places)

        messages = [
            message(sweep, 0, X_BOTH, 3, x_other),
            message(sweep, 1, T_AHEAD, 3, t_prior),
            message(sweep, 2, T_BEHIND, 3, t_next),
            message(sweep, 3, Y_AHEAD, 3, y_prior),
            message(sweep, 4, Y_BEHIND, 3, y_next),
            message(sweep, 5, Z_BOTH, 6, z_other),
        ]
        if before_send is not None:
            before_send()
        for copy in messages:
            copy.start()
            started.append(copy)
        if while_waiting is not None:
            while_waiting()

        ahead_moved = {mu: lane_roll(ahead[mu], -STRIDE[mu]) for mu in (1, 2, 3)}
        behind_moved = {mu: lane_roll(behind[mu], STRIDE[mu]) for mu in (1, 2, 3)}
        zero = jnp.zeros((3, 8, 128), F32)
        summed = [(zero, zero)] * 4

        def finish(summed, mu, from_ahead, from_behind):
            summed = lift(summed, link_times(links, mu, from_ahead, False), mu, -1)
            return lift(summed, from_behind, mu, 1)

        messages[5].wait_recv()
        summed = finish(
            summed,
            1,
            merge_slots(ahead_moved[1], recv[Z_BOTH : Z_BOTH + 3], 1, True, places),
            merge_slots(behind_moved[1], recv[Z_BOTH + 3 : Z_BOTH + 6], 1, False, places),
        )
        messages[3].wait_recv()
        messages[4].wait_recv()
        summed = finish(
            summed,
            2,
            merge_slots(ahead_moved[2], recv[Y_AHEAD : Y_AHEAD + 3], 2, True, places),
            merge_slots(behind_moved[2], recv[Y_BEHIND : Y_BEHIND + 3], 2, False, places),
        )
        messages[1].wait_recv()
        messages[2].wait_recv()
        summed = finish(
            summed,
            0,
            merge_time(t_ahead_state, recv[T_AHEAD : T_AHEAD + 3], True, places),
            merge_time(t_behind_state, recv[T_BEHIND : T_BEHIND + 3], False, places),
        )
        messages[0].wait_recv()
        x_recv = recv[X_BOTH : X_BOTH + 3]
        x_from_ahead = choose(places.block == 3, row_roll(x_recv, 3), row_roll(x_ahead, -1))
        x_from_behind = choose(places.block == 0, row_roll(x_recv, -3), row_roll(x_behind, 1))
        summed = finish(
            summed,
            3,
            merge_slots(ahead_moved[3], x_from_ahead, 3, True, places),
            merge_slots(behind_moved[3], x_from_behind, 3, False, places),
        )

        result = []
        for chirality in range(2):
            pair = summed[2 * chirality : 2 * chirality + 2]
            out_real = out_imag = None
            for column in range(6):
                c_real = clover[chirality, 0, :, column]
                c_imag = clover[chirality, 1, :, column]
                v_real = pair[column // 3][0][column % 3][None]
                v_imag = pair[column // 3][1][column % 3][None]
                term_real = c_real * v_real - c_imag * v_imag
                term_imag = c_real * v_imag + c_imag * v_real
                out_real = term_real if out_real is None else out_real + term_real
                out_imag = term_imag if out_imag is None else out_imag + term_imag
            result.append((out_real[:3], out_imag[:3]))
            result.append((out_real[3:], out_imag[3:]))
        return tiles_of(result)

    loads[0].wait()
    source = source_ref[...]
    scaled[...] = fine_relax * source
    loads[1].wait()
    links[...] = links_raw[...].astype(F32).reshape(links.shape)

    def convert():
        loads[2].wait()
        clover[...] = (fine_relax * kappa_value) * clover_raw[...].astype(F32).reshape(clover.shape)
        loads[3].wait()
        for pair in range(6):
            both = vectors_raw[:, pair].astype(F32).reshape(32, 2, 8, 128)
            for side in range(2):
                place = (2 * pair + side) * 128
                matrix[:, place : place + 128] = both[:, side].reshape(256, 128).astype(BF16)

    def enter():
        pl.semaphore_wait(barrier, 6)

    psi = scaled[...]
    psi = (1.0 - fine_relax) * psi + scaled[...] + clover_hopping(0, psi, enter, convert)

    change = clover_hopping(1, psi)
    residual = source_ref[...] - psi + (1.0 / fine_relax) * change

    stacked = jnp.stack([residual[:12], residual[12:]], axis=1).reshape(12, 16, 128).astype(BF16)
    flat = jnp.concatenate([stacked[c] for c in range(12)], axis=1)
    products = lax.dot_general(
        flat, matrix[...], (((1,), (1,)), ((), ())), preferred_element_type=F32
    )
    wide_row = lax.broadcasted_iota(jnp.int32, (16, 256), 0)
    wide_lane = lax.broadcasted_iota(jnp.int32, (16, 256), 1)
    same_row = wide_row % 8 == wide_lane % 8
    products = jnp.where(same_row, products, 0.0)
    high = products.astype(BF16)
    low = (products - high.astype(F32)).astype(BF16)
    gather_row = lax.broadcasted_iota(jnp.int32, (256, 128), 0)
    gather_lane = lax.broadcasted_iota(jnp.int32, (256, 128), 1)
    gather = (gather_lane == gather_row // 16 + 16 * ((gather_row // 8) % 2)).astype(F32).astype(BF16)
    sums = jnp.dot(high, gather, preferred_element_type=F32) + jnp.dot(
        low, gather, preferred_element_type=F32
    )
    with_real, with_imag = sums[:8], sums[8:]
    narrow = places.lane < 16
    coarse_real = jnp.where(narrow, with_real + lane_roll(with_imag, -16), 0.0)
    coarse_imag = jnp.where(narrow, with_imag - lane_roll(with_real, -16), 0.0)
    coarse_real = coarse_real + row_roll(coarse_real, 4)
    coarse_imag = coarse_imag + row_roll(coarse_imag, 4)

    own = jnp.where(places.half == 0, coarse_real, coarse_imag)
    coarse_send[...] = own
    coarse_messages = []
    for number, target in enumerate((x_other, t_prior, t_next, y_prior, y_next, z_other)):
        copy = pltpu.make_async_remote_copy(
            src_ref=coarse_send,
            dst_ref=coarse_recv.at[number],
            send_sem=coarse_send_sem.at[number],
            recv_sem=coarse_recv_sem.at[number],
            device_id=target,
            device_id_type=pl.DeviceIdType.MESH,
        )
        copy.start()
        coarse_messages.append(copy)
        started.append(copy)
    loads[4].wait()

    accumulated = [jnp.zeros((8, 8, 16), F32), jnp.zeros((8, 8, 16), F32)]

    def add_hop(number, tile):
        tile = coarse_relax * tile
        swapped = row_roll(tile, 4)
        e_real = jnp.where(places.half == 0, tile, swapped)[:, :16][None]
        e_imag = jnp.where(places.half == 0, swapped, tile)[:, :16][None]
        h_real, h_imag = hops_ref[number, 0], hops_ref[number, 1]
        accumulated[0] = accumulated[0] + (h_real * e_real - h_imag * e_imag)
        accumulated[1] = accumulated[1] + (h_real * e_imag + h_imag * e_real)

    coarse_messages[5].wait_recv()
    z_tile = coarse_recv[5]
    add_hop(2, z_tile)
    add_hop(3, z_tile)
    coarse_messages[3].wait_recv()
    add_hop(4, coarse_recv[3])
    coarse_messages[4].wait_recv()
    add_hop(5, coarse_recv[4])
    coarse_messages[1].wait_recv()
    add_hop(0, coarse_recv[1])
    coarse_messages[2].wait_recv()
    add_hop(1, coarse_recv[2])
    coarse_messages[0].wait_recv()
    x_tile = coarse_recv[0]
    add_hop(6, jnp.where(places.block == 3, row_roll(x_tile, 3), row_roll(own, -1)))
    add_hop(7, jnp.where(places.block == 0, row_roll(x_tile, -3), row_roll(own, 1)))

    def gathered(values):
        totals = jnp.sum(values, axis=-1, keepdims=True)
        spread = jnp.zeros((8, 128), F32)
        for pair in range(8):
            column = jnp.broadcast_to(totals[pair], (8, 128))
            spread = jnp.where(places.lane // 2 == pair, column, spread)
        return jnp.where(places.lane % 2 == places.half, spread, row_roll(spread, 4))

    first_real, first_imag = coarse_relax * coarse_real, coarse_relax * coarse_imag
    error_real = first_real + coarse_relax * (
        coarse_real - (first_real - gathered(accumulated[0]))
    )
    error_imag = first_imag + coarse_relax * (
        coarse_imag - (first_imag - gathered(accumulated[1]))
    )
    coarse_ref[0] = error_real[:4, :16]
    coarse_ref[1] = error_imag[:4, :16]

    error_real = jnp.where(narrow, error_real, 0.0)
    error_imag = jnp.where(narrow, error_imag, 0.0)
    weights = jnp.concatenate(
        [error_real - lane_roll(error_imag, 16), error_imag + lane_roll(error_real, 16)], axis=0
    ).astype(BF16)
    scatter_row = lax.broadcasted_iota(jnp.int32, (128, 256), 0)
    scatter_lane = lax.broadcasted_iota(jnp.int32, (128, 256), 1)
    scatter = (
        (scatter_row == scatter_lane // 16 + 16 * ((scatter_lane // 8) % 2)).astype(F32).astype(BF16)
    )
    spread_weights = jnp.dot(weights, scatter, preferred_element_type=F32)
    spread_weights = jnp.where(same_row, spread_weights, 0.0).astype(BF16)
    correction = jnp.dot(spread_weights, matrix[...], preferred_element_type=F32)
    correction = jnp.concatenate(
        [correction[:8, 128 * c : 128 * c + 128][None] for c in range(12)]
        + [correction[8:, 128 * c : 128 * c + 128][None] for c in range(12)],
        axis=0,
    )
    psi = psi + correction

    for sweep in (2, 3):
        psi = (1.0 - fine_relax) * psi + scaled[...] + clover_hopping(sweep, psi)
    out_ref[...] = psi

    for copy in started:
        copy.wait_send()


def rows_of_eight(values):
    count = values.size // 1024
    return values.reshape(count, 4, 2, 128).transpose(0, 2, 1, 3).reshape(count, 8, 128)


def local(source, gauge_links, clover_inverse, vectors, coarse_hops):
    source_tiles = rows_of_eight(source)
    link_tiles = rows_of_eight(gauge_links).reshape(36, 16, 128)
    clover_tiles = rows_of_eight(clover_inverse).reshape(72, 16, 128)
    vector_tiles = rows_of_eight(vectors).reshape(32, 6, 16, 128)
    hop_tiles = (
        coarse_hops.reshape(8, 2, 16, 16, 4).transpose(0, 1, 2, 4, 3).reshape(8, 2, 8, 8, 16)
    )
    out, coarse = pl.pallas_call(
        kernel,
        out_shape=(
            jax.ShapeDtypeStruct((24, 8, 128), F32),
            jax.ShapeDtypeStruct((2, 4, 16), F32),
        ),
        in_specs=[pl.BlockSpec(memory_space=pltpu.HBM)] * 5,
        out_specs=(
            pl.BlockSpec(memory_space=pltpu.VMEM),
            pl.BlockSpec(memory_space=pltpu.VMEM),
        ),
        scratch_shapes=[
            pltpu.VMEM((24, 8, 128), F32),
            pltpu.VMEM((36, 16, 128), BF16),
            pltpu.VMEM((72, 16, 128), BF16),
            pltpu.VMEM((32, 6, 16, 128), BF16),
            pltpu.VMEM((8, 2, 8, 8, 16), F32),
            pltpu.VMEM((4, 2, 3, 3, 8, 128), F32),
            pltpu.VMEM((2, 2, 6, 6, 8, 128), F32),
            pltpu.VMEM((256, 1536), BF16),
            pltpu.VMEM((24, 8, 128), F32),
            pltpu.VMEM((4, TILES, 8, 128), F32),
            pltpu.VMEM((4, TILES, 8, 128), F32),
            pltpu.VMEM((8, 128), F32),
            pltpu.VMEM((6, 8, 128), F32),
            pltpu.SemaphoreType.DMA((5,)),
            pltpu.SemaphoreType.DMA((4, 6)),
            pltpu.SemaphoreType.DMA((4, 6)),
            pltpu.SemaphoreType.DMA((6,)),
            pltpu.SemaphoreType.DMA((6,)),
        ],
        compiler_params=pltpu.CompilerParams(
            collective_id=0, has_side_effects=True, vmem_limit_bytes=48 * 1024 * 1024
        ),
    )(source_tiles, link_tiles, clover_tiles, vector_tiles, hop_tiles)
    solution_out = (
        out.reshape(24, 2, 4, 128).transpose(0, 2, 1, 3).reshape(2, 4, 3, 1, 1, 1, 4, 256)
    )
    coarse_out = coarse.transpose(0, 2, 1).reshape(2, 16, 1, 1, 1, 4)
    return solution_out, coarse_out


def solution(mesh):
    return jax.shard_map(
        local,
        mesh=mesh,
        in_specs=(
            P(None, None, None, "ta", "gz", "gy", "gx", None),
            P(None, None, None, None, "ta", "gz", "gy", "gx", None),
            P(None, None, None, None, "ta", "gz", "gy", "gx", None),
            P(None, None, None, None, "ta", "gz", "gy", "gx", None),
            P(None, None, None, None, "ta", "gz", "gy", "gx"),
        ),
        out_specs=(
            P(None, None, None, "ta", "gz", "gy", "gx", None),
            P(None, None, "ta", "gz", "gy", "gx"),
        ),
        check_vma=False,
    )
```

time: 418 us -> 37.1 us (0.09); the launches traced: 410 us -> 36.8 us
  local copies, waits for them, and re-layouts: 223 us -> 6.17 us
  starting transfers between devices: 50.7 us -> 0 us
  other arithmetic: 44.4 us -> 0 us
  blocking collectives: 34 us -> 0 us
  Pallas kernels: 0 us -> 30 us
  matrix products: 23.5 us -> 0 us
  between operations: 19.9 us -> 0.65 us
  waiting for transfers between devices: 14.5 us -> 0 us
    another operation x118 -> x0, local copies, waits for them, and re-layouts: 100 us -> none  [the longest x56 40.7 us: colour(): jnp.stack([jnp.sum(real_part * vector_real - imag_part * vector_imag, axi...]
    slice x151 -> x0, local copies, waits for them, and re-layouts: 69.8 us -> none  [the longest x24 34.5 us: hopping(): forward_half[..., 1:, :]]
    ppermute x34 -> x0, starting transfers between devices: 50.6 us -> none  [the longest x17 26.2 us: extended(): lax.ppermute(lax.slice_in_dim(block, block.shape[dim] - width, None, axis...]
    all_gather x1 -> x0, blocking collectives: 34 us -> none  [local(): lax.all_gather(coarse_source[None], ('gz', 'gy', 'gx'), axis=0, tiled=True)]
    pallas_call x0 -> x1, Pallas kernels: none -> 30 us  [local(): pl.pallas_call(kernel, out_shape=(jax.ShapeDtypeStruct((24, 8, 128), F32)...]
    reshape x26 -> x0, local copies, waits for them, and re-layouts: 25.8 us -> none  [the longest x2 10.8 us: regroup(): reshaped = values.reshape(group_sizes + trailing)]
    dot_general x66 -> x0, matrix products: 23.5 us -> none  [the longest x64 21.7 us: apply_spin(): jnp.tensordot(jnp.asarray(spin_table), flattened, axes=1, precision=lax.P...]
    mul x48 -> x0, local copies, waits for them, and re-layouts: 18.5 us -> none  [the longest x24 9.56 us: colour(): real_part * vector_real - imag_part * vector_imag]
  transfers between devices with their start and end apart: 35 -> 0, of which waited for: 5 -> 0; matrix products, arithmetic and copies ran while one was open for 54% -> 0% of each run, Pallas kernels for 0% -> 0%
where the time goes in v1:
time: 37.1 us; the launch traced here: 36.8 us
  Pallas kernels  30 us (81%)
  local copies, waits for them, and re-layouts  6.17 us (17%)
  between operations  0.65 us (2%)
    pallas_call x1, Pallas kernels, local(): pl.pallas_call(kernel, out_shape=(jax.ShapeDtypeStruct((24, 8, 128), F32)...  30 us
    unnamed x12, local copies, waits for them, and re-layouts  6.17 us

profile of v1, /device:TPU:24, one launch (start us, length us, event | category | flops | bytes accessed | tf_op | source)
XLA Modules:
  0.0 36.8 jit_solution(3469308104356776989)
XLA Ops:
  0.6 0.0 copy-start
  0.6 1.1 %copy-done = bf16[16,2,4,3,1,1,1,4,256]{8,7,6,5,4,3,2,1,0:T(4,128)(2,1)S(1)} copy-done((bf16[16,2,4,3,1,1,1,4,256]{8,7,6,5,4,3,2,1,0:T(4,128)(2,1)S(1)}, bf16[16,2,4,3,1,1,1,4,256]{8,7,6,5,4,3,2,1,0:T(4,128)(2,1)}, u32[]{:S(2)}) %copy-start) | copy-done | bytes 786456
  1.8 0.0 copy-start.1
  1.8 1.0 %copy-done.1 = f32[8,2,16,16,1,1,1,4]{3,7,6,5,4,2,1,0:T(4,128)S(1)} copy-done((f32[8,2,16,16,1,1,1,4]{3,7,6,5,4,2,1,0:T(4,128)S(1)}, f32[8,2,16,16,1,1,1,4]{3,7,6,5,4,2,1,0:T(4,128)}, u32[]{:S(2)}) %copy-start.1) | copy-done | bytes 65560
  2.8 0.0 copy-start.2
  2.8 1.0 %copy-done.2 = bf16[2,2,6,6,1,1,1,4,256]{8,7,6,5,4,3,2,1,0:T(4,128)(2,1)S(1)} copy-done((bf16[2,2,6,6,1,1,1,4,256]{8,7,6,5,4,3,2,1,0:T(4,128)(2,1)S(1)}, bf16[2,2,6,6,1,1,1,4,256]{8,7,6,5,4,3,2,1,0:T(4,128)(2,1)}, u32[]{:S(2)}) %copy-start.2) | copy-done | bytes 294936
  3.8 0.0 copy-start.3
  3.8 0.9 %copy-done.3 = bf16[4,2,3,3,1,1,1,4,256]{8,7,6,5,4,3,2,1,0:T(4,128)(2,1)S(1)} copy-done((bf16[4,2,3,3,1,1,1,4,256]{8,7,6,5,4,3,2,1,0:T(4,128)(2,1)S(1)}, bf16[4,2,3,3,1,1,1,4,256]{8,7,6,5,4,3,2,1,0:T(4,128)(2,1)}, u32[]{:S(2)}) %copy-start.3) | copy-done | bytes 147480
  4.7 0.0 copy-start.4
  4.7 0.9 %copy-done.4 = f32[2,4,3,1,1,1,4,256]{7,6,5,4,3,2,1,0:T(4,128)S(1)} copy-done((f32[2,4,3,1,1,1,4,256]{7,6,5,4,3,2,1,0:T(4,128)S(1)}, f32[2,4,3,1,1,1,4,256]{7,6,5,4,3,2,1,0:T(4,128)}, u32[]{:S(2)}) %copy-start.4) | copy-done | bytes 98328
  5.6 30.0 %shard_map.68 = (f32[24,8,128]{2,1,0:T(8,128)S(1)}, f32[2,4,16]{2,1,0:T(4,128)S(1)}) custom-call(f32[24,8,128]{2,1,0:T(8,128)S(1)} %bitcast.37, bf16[36,16,128]{2,1,0:T(8,128)(2,1)S(1)} %bitcast.36, bf16[72,16,128]{2,1,0:T(8,128)(2,1)S(1)} %bitcast.35, bf16[32,6,16,128]{3,2,1,0:T(8,128)(2,1)S(1)} %bitcast.33, f32[8,2,8,8,16]{4,3,2,1,0:T(8,128)S(1)} %bitcast.34), custom_call_target="tpu_custom_call" | custom-call | tf_op jit(solution)/shard_map/pallas_call | solution.py:476
  35.5 0.6 %copy.14 = f32[2,4,3,1,1,1,4,256]{7,6,5,4,3,2,1,0:T(4,128)} copy(f32[2,4,3,1,1,1,4,256]{7,6,5,4,3,2,1,0:T(4,128)S(1)} %bitcast.38) | data formatting | bytes 196608
  36.2 0.6 %copy.15 = f32[2,16,1,1,1,4]{1,5,4,3,2,0:T(4,128)} copy(f32[2,16,1,1,1,4]{1,5,4,3,2,0:T(4,128)S(1)} %bitcast.39) | data formatting | bytes 1024
Async XLA Ops:
  0.6 1.1 %copy-start = (bf16[16,2,4,3,1,1,1,4,256]{8,7,6,5,4,3,2,1,0:T(4,128)(2,1)S(1)}, bf16[16,2,4,3,1,1,1,4,256]{8,7,6,5,4,3,2,1,0:T(4,128)(2,1)}, u32[]{:S(2)}) copy-start(bf16[16,2,4,3,1,1,1,4,256]{8,7,6,5,4,3,2,1,0:T(4,128)(2,1)} %param.8) | copy-start | bytes 2359300
  1.8 1.0 %copy-start.1 = (f32[8,2,16,16,1,1,1,4]{3,7,6,5,4,2,1,0:T(4,128)S(1)}, f32[8,2,16,16,1,1,1,4]{3,7,6,5,4,2,1,0:T(4,128)}, u32[]{:S(2)}) copy-start(f32[8,2,16,16,1,1,1,4]{3,7,6,5,4,2,1,0:T(4,128)} %param.9) | copy-start | bytes 196612
  2.8 1.0 %copy-start.2 = (bf16[2,2,6,6,1,1,1,4,256]{8,7,6,5,4,3,2,1,0:T(4,128)(2,1)S(1)}, bf16[2,2,6,6,1,1,1,4,256]{8,7,6,5,4,3,2,1,0:T(4,128)(2,1)}, u32[]{:S(2)}) copy-start(bf16[2,2,6,6,1,1,1,4,256]{8,7,6,5,4,3,2,1,0:T(4,128)(2,1)} %param.7) | copy-start | bytes 884740
  3.8 0.9 %copy-start.3 = (bf16[4,2,3,3,1,1,1,4,256]{8,7,6,5,4,3,2,1,0:T(4,128)(2,1)S(1)}, bf16[4,2,3,3,1,1,1,4,256]{8,7,6,5,4,3,2,1,0:T(4,128)(2,1)}, u32[]{:S(2)}) copy-start(bf16[4,2,3,3,1,1,1,4,256]{8,7,6,5,4,3,2,1,0:T(4,128)(2,1)} %param.6) | copy-start | bytes 442372
  4.7 0.9 %copy-start.4 = (f32[2,4,3,1,1,1,4,256]{7,6,5,4,3,2,1,0:T(4,128)S(1)}, f32[2,4,3,1,1,1,4,256]{7,6,5,4,3,2,1,0:T(4,128)}, u32[]{:S(2)}) copy-start(f32[2,4,3,1,1,1,4,256]{7,6,5,4,3,2,1,0:T(4,128)} %param.5) | copy-start | bytes 294916
